TPU v7x, 32 devices: a whole 2x2x4 slice. The times are simulated.
32 devices in a mesh: enc: 4 (over x, core), fsdp: 8 (over z, y).
Axes of the slice: x: 2, y: 2, z: 4, core: 2. Of those that a mesh axis runs over, the one named last changes fastest.
Arguments:
- enc_features: bfloat16 [8, 8, 1024, 512], P(None, 'enc', 'fsdp'), may hold values from -6 to 6
- enc_gain: float32 [1, 512], replicated, may hold values from 0.1 to 1.9
- enc_kernel: bfloat16 [1, 3, 512, 512], replicated, may hold values from -0.15625 to 0.15625
- out_kernel: bfloat16 [512, 16], replicated, may hold values from -0.25 to 0.25
- clip_start: int32 [8], replicated, may hold values from 0 to 3
- assign: int32 [8], replicated, may hold values from 0 to 7, each once
- embed_weight: bfloat16 [3072, 64], P('fsdp'), may hold values from -0.75 to 0.75
- mod_shift: float32 [8, 3072], P('fsdp'), may hold values from -3 to 3
- mod_scale: float32 [8, 3072], P('fsdp'), may hold values from -3 to 3
- value_weight: bfloat16 [3072, 1536], P('fsdp'), may hold values from -0.109375 to 0.109375
- value_cotangent: bfloat16 [8, 8, 256, 1536], P('fsdp', 'enc'), may hold values from -6 to 6
Outputs:
- values: bfloat16 [8, 8, 256, 1536], P('fsdp', 'enc')
- grad_value: float32 [3072, 1536], P(('enc', 'fsdp'))
- grad_embed: float32 [3072, 64], P(('enc', 'fsdp'))
Inputs may be any that keep to these rules, and one draw needn't show every extreme that they name: Sample s is made from clip assign[s]; every clip is taken by exactly one sample.
All inputs are finite; a program needn't handle non-finite values.
Results may differ from a plain program's by a relative error of at most 0.025.
Values may be sent and summed in bfloat16 or wider, within the bound.
A program may use at most 192 MiB of HBM per device.

v0:
```python
import jax
import jax.numpy as jnp
from jax import lax
from jax.sharding import PartitionSpec as P


def from_behind(x, axis, by):
    size = lax.axis_size(axis)
    pairs = [(i, i + by) for i in range(size) if 0 <= i + by < size]
    return lax.ppermute(x, axis, pairs)


def channel_norm(activation, gain_row):
    scaling = lax.rsqrt(jnp.mean(activation * activation, axis=-1, keepdims=True) + 1e-06)
    return activation * scaling * gain_row


def local(
    enc_features,
    enc_gain,
    enc_kernel,
    out_kernel,
    clip_start,
    assign,
    embed_weight,
    mod_shift,
    mod_scale,
    value_weight,
    value_cotangent,
):
    clip_count, frame_count, pixel_count, channels = enc_features.shape
    first_frame = lax.axis_index("enc") * frame_count
    frame_ids = first_frame + jnp.arange(frame_count, dtype=jnp.int32)
    live_mask = (frame_ids[None, :] >= clip_start[:, None]).astype(jnp.float32)[:, :, None, None]
    stored = enc_features
    activation = stored.astype(jnp.float32)
    normed = (live_mask * channel_norm(activation, enc_gain[0])).astype(jnp.bfloat16)
    before = from_behind(normed, "enc", 1)
    padded = jnp.concatenate([before, normed], axis=1)
    convolved = jnp.zeros(activation.shape, jnp.float32)
    for offset in range(3):
        window = padded[:, offset : offset + frame_count].reshape(-1, channels)
        convolved = convolved + jnp.dot(
            window, enc_kernel[0, offset], preferred_element_type=jnp.float32
        ).reshape(activation.shape)
    stored = (activation + jax.nn.silu(convolved)).astype(jnp.bfloat16)
    latent = jnp.dot(stored.reshape(-1, channels), out_kernel, preferred_element_type=jnp.float32)
    latent = latent.reshape(clip_count, frame_count, pixel_count, out_kernel.shape[1])
    latent = (latent * live_mask).astype(jnp.bfloat16)
    latent = latent.reshape(clip_count, frame_count, pixel_count // 4, 4 * out_kernel.shape[1])
    everything = lax.all_gather(latent, "fsdp", axis=2, tiled=True)
    mine = lax.dynamic_slice_in_dim(everything, assign[lax.axis_index("fsdp")], 1, 0)
    token_rows = mine.reshape(-1, mine.shape[-1])
    embed_full, weight_full = (
        lax.all_gather(embed_weight, "fsdp", axis=0, tiled=True),
        lax.all_gather(value_weight, "fsdp", axis=0, tiled=True),
    )
    mixed = lax.dot_general(
        token_rows, embed_full, (((1,), (1,)), ((), ())), preferred_element_type=jnp.float32
    )
    row_mean = jnp.mean(mixed, axis=-1, keepdims=True)
    centred = mixed - row_mean
    row_var = jnp.mean(centred * centred, axis=-1, keepdims=True)
    inv_std = lax.rsqrt(row_var + 1e-06)
    unit = centred * inv_std
    modulated = (unit * (1.0 + mod_scale) + mod_shift).astype(jnp.bfloat16)
    projected = jnp.dot(modulated, weight_full, preferred_element_type=jnp.float32).astype(
        jnp.bfloat16
    )
    cot_rows = value_cotangent.reshape(-1, value_cotangent.shape[-1])
    weight_back = lax.all_gather(value_weight, "fsdp", axis=0, tiled=True)
    grad_mod = lax.dot_general(
        cot_rows, weight_back, (((1,), (1,)), ((), ())), preferred_element_type=jnp.float32
    )
    grad_unit = grad_mod * (1.0 + mod_scale)
    grad_mixed = inv_std * (
        grad_unit
        - jnp.mean(grad_unit, axis=-1, keepdims=True)
        - unit * jnp.mean(grad_unit * unit, axis=-1, keepdims=True)
    )
    grad_bf = grad_mixed.astype(jnp.bfloat16)
    grad_w = lax.dot_general(
        modulated, cot_rows, (((0,), (0,)), ((), ())), preferred_element_type=jnp.float32
    )
    grad_e = lax.dot_general(
        grad_bf, token_rows, (((0,), (0,)), ((), ())), preferred_element_type=jnp.float32
    )
    part_w, part_e = (
        lax.psum_scatter(
            grad_w.astype(jnp.bfloat16), "enc", scatter_dimension=0, tiled=True
        ).astype(jnp.float32),
        lax.psum_scatter(
            grad_e.astype(jnp.bfloat16), "enc", scatter_dimension=0, tiled=True
        ).astype(jnp.float32),
    )
    grad_value, grad_embed = (
        lax.psum_scatter(
            part_w.astype(jnp.bfloat16), "fsdp", scatter_dimension=0, tiled=True
        ).astype(jnp.float32),
        lax.psum_scatter(
            part_e.astype(jnp.bfloat16), "fsdp", scatter_dimension=0, tiled=True
        ).astype(jnp.float32),
    )
    return (projected.reshape(value_cotangent.shape), grad_value, grad_embed)


def solution(mesh):
    in_specs = (
        P(None, "enc", "fsdp", None),
        P(),
        P(),
        P(),
        P(),
        P(),
        P("fsdp", None),
        P("fsdp", None),
        P("fsdp", None),
        P("fsdp", None),
        P("fsdp", "enc", None, None),
    )
    out_specs = (P("fsdp", "enc", None, None), P(("enc", "fsdp"), None), P(("enc", "fsdp"), None))
    return jax.shard_map(local, mesh=mesh, in_specs=in_specs, out_specs=out_specs, check_vma=False)
```

profile of v0, /device:TPU:0, one launch (start us, length us, event | category | flops | bytes accessed | tf_op | source)
XLA Modules:
  0.0 430.4 jit_solution(7311882795879825856)
XLA Ops:
  7.2 0.0 copy-start
  7.2 0.0 copy-start.7
  7.2 0.0 copy-start.3
  7.2 0.0 all-gather.2.cloned.1.call-start
  7.2 0.7 all-gather.2.cloned.1.call-update
  7.9 0.0 reduce-scatter.11.cloned.1.call-start
  8.0 0.7 compare_convert_fusion
  8.7 2.1 fusion
  10.8 3.7 fusion.3
  14.5 3.7 collective-permute-start
  18.2 0.0 copy-done.7
  18.2 0.6 dynamic_slice.6
  20.8 0.0 copy-done.3
  20.8 33.8 %all_gather.11 = bf16[3072,64]{0,1:T(8,128)(2,1)S(1)} all-gather(bf16[384,64]{0,1:T(8,128)(2,1)S(1)} %copy-done.3), channel_id=1, replica_groups=mesh['enc'=4,'fsdp'=8] {'fsdp'}, dimensions={0}, use_global_device_ids=true | all-gather | bytes 442368 | tf_op jit(solution)/shard_map/all_gather | solution.py:55
  54.6 0.0 copy-start.4
  54.6 5.0 %fusion.12 = f32[8,2,128,512]{3,2,1,0:T(8,128)} fusion(bf16[8,2,128,512]{3,2,1,0:T(8,128)(2,1)} %fusion.3, bf16[1,3,512,512]{3,2,1,0:T(8,128)(2,1)} %param.13), kind=kOutput, calls=%fused_computation.24 | convolution fusion | flops 1073741824 | bytes 6815744 | tf_op jit(solution)/shard_map/dot_general | solution.py:43
  59.6 0.0 copy-done.4
  59.6 0.0 copy-start.5
  59.6 0.0 collective-permute-done
  59.6 4.9 %fusion.5 = f32[8,2,128,512]{3,2,1,0:T(8,128)} fusion(bf16[8,2,128,512]{3,2,1,0:T(8,128)(2,1)} %fusion.3, bf16[8,2,128,512]{3,2,1,0:T(8,128)(2,1)} %collective-permute-done, bf16[1,3,512,512]{3,2,1,0:T(8,128)(2,1)} %param.13), kind=kOutput, calls=%fused_computation.15 | convolution fusion | flops 1082130432 | bytes 8912896 | tf_op jit(solution)/shard_map/dot_general | solution.py:43
  64.5 0.0 copy-done.5
  64.5 7.3 %fusion.11 = bf16[8,2,128,16]{2,3,1,0:T(8,128)(2,1)S(1)} fusion(bf16[8,2,128,512]{3,2,1,0:T(8,128)(2,1)} %param.11, f32[8,2,128,512]{3,2,1,0:T(8,128)} %fusion.12, f32[8,2,128,512]{3,2,1,0:T(8,128)} %fusion.5, bf16[8,2,128,512]{3,2,1,0:T(8,128)(2,1)} %collective-permute-done, bf16[1,3,512,512]{3,2,1,0:T(8,128)(2,1)} %param.13, ...), kind=kOutput, calls=%fused_computation.23 | convolution fusion | flops 1116798976 | bytes 13189184 | tf_op jit(solution)/shard_map/dot_general | solution.py:47
  71.8 0.3 copy.15
  72.1 0.3 reshape.96
  72.4 38.3 %all_gather.10 = bf16[8,2,256,64]{3,2,1,0:T(8,128)(2,1)S(1)} all-gather(bf16[8,2,32,64]{3,2,1,0:T(8,128)(2,1)S(1)} %reshape.96), channel_id=1, replica_groups=mesh['enc'=4,'fsdp'=8] {'fsdp'}, dimensions={2}, use_global_device_ids=true | all-gather | bytes 589824 | tf_op jit(solution)/shard_map/all_gather | solution.py:51
  110.7 1.0 fusion.24
  111.7 0.0 copy-start.1
  111.7 2.6 copy-done.1
  114.3 0.8 multiply_reduce_fusion.1
  115.1 56.7 %all-gather.2.cloned.1.call-done = bf16[3072,1536]{1,0:T(8,128)(2,1)} async-done(((bf16[384,1536]{1,0:T(8,128)(2,1)}), bf16[3072,1536]{1,0:T(8,128)(2,1)}) %all-gather.2.cloned.1.call-update) | async-done | bytes 9437200 | tf_op jit(solution)/shard_map/all_gather | solution.py:56
  171.8 0.0 copy-done
  171.8 0.0 copy-start.2
  171.8 10.6 %multiply_reduce_fusion.2 = (f32[512]{0:T(512)S(1)}, f32[512]{0:T(512)S(1)}, f32[512,3072]{1,0:T(8,128)S(1)}) fusion(f32[3072]{0:T(1024)S(1)} %bitcast.50, f32[512]{0:T(512)S(1)} %add_rsqrt_fusion.1, f32[512,3072]{1,0:T(8,128)} %copy-done.1, f32[512]{0:T(512)S(1)} %broadcast_multiply_fusion.2, bf16[512,1536]{1,0:T(8,128)(2,1)S(1)} %bitcast.47, ...), kind=kOutput, calls=%fused_computation.9 | convolution fusion | flops 4841274368 | bytes 23613440 | tf_op jit(solution)/shard_map/dot_general | solution.py:72
  182.3 0.0 copy-done.2
  182.3 0.0 copy-start.6
  182.4 2.8 convolution_convert_fusion.1
  185.2 0.0 reduce-scatter.11.cloned.1.call-update
  185.2 0.0 reduce-scatter.7.cloned.1.call-start
  185.2 0.0 copy-done.6
  185.2 11.2 %convolution_convert_fusion = bf16[3072,1536]{1,0:T(8,128)(2,1)} fusion(bf16[512,1536]{1,0:T(8,128)(2,1)S(1)} %bitcast.46, f32[512,3072]{1,0:T(8,128)} %copy-done.1, f32[3072]{0:T(1024)S(1)} %bitcast.55, f32[3072]{0:T(1024)S(1)} %bitcast.52, f32[512]{0:T(512)S(1)} %add_rsqrt_fusion.1, f32[512]{0:T(512)S(1)} %broadcast_multiply_fusion.2), kind=kOutput, calls=%fused_computation | convolution fusion | flops 4844421120 | bytes 17330176 | tf_op jit(solution)/shard_map/dot_general | solution.py:82
  196.4 0.0 reduce-scatter.7.cloned.1.call-update
  196.4 0.0 reduce-scatter.13.cloned.1.call-start
  196.5 8.3 %reduce-scatter.11.cloned.1.call-done = bf16[768,64]{0,1:T(8,128)(2,1)} async-done(((bf16[3072,64]{0,1:T(8,128)(2,1)}), bf16[768,64]{0,1:T(8,128)(2,1)}) %reduce-scatter.11.cloned.1.call-update) | async-done | bytes 98320 | tf_op jit(solution)/shard_map/reduce_scatter | solution.py:92
  204.8 1.7 copy.20
  206.5 0.0 reduce-scatter.13.cloned.1.call-update
  206.5 0.0 reduce-scatter.9.cloned.1.call-start
  206.6 79.3 %reduce-scatter.7.cloned.1.call-done = bf16[768,1536]{1,0:T(8,128)(2,1)} async-done(((bf16[3072,1536]{1,0:T(8,128)(2,1)}), bf16[768,1536]{1,0:T(8,128)(2,1)}) %reduce-scatter.7.cloned.1.call-update) | async-done | bytes 2359312 | tf_op jit(solution)/shard_map/reduce_scatter | solution.py:89
  285.8 0.0 reduce-scatter.9.cloned.1.call-update
  285.9 11.0 %convolution_convert_fusion.2 = bf16[512,1536]{1,0:T(8,128)(2,1)} fusion(bf16[3072,1536]{1,0:T(8,128)(2,1)} %all-gather.2.cloned.1.call-done, f32[512,3072]{1,0:T(8,128)} %copy-done.1, f32[3072]{0:T(1024)S(1)} %bitcast.56, f32[3072]{0:T(1024)S(1)} %bitcast.53, f32[512]{0:T(512)S(1)} %add_rsqrt_fusion.1, f32[512]{0:T(512)S(1)} %broadcast_multiply_fusion.2), kind=kOutput, calls=%fused_computation.20 | convolution fusion | flops 4840488960 | bytes 17330176 | tf_op jit(solution)/shard_map/dot_general | solution.py:67
  296.8 53.8 %reduce-scatter.13.cloned.1.call-done = bf16[96,64]{1,0:T(8,128)(2,1)} async-done(((bf16[768,64]{1,0:T(8,128)(2,1)}), bf16[96,64]{1,0:T(8,128)(2,1)}) %reduce-scatter.13.cloned.1.call-update) | async-done | bytes 12304
  350.6 0.8 copy.21
  351.4 0.6 convert_element_type.55
  352.1 69.9 %reduce-scatter.9.cloned.1.call-done = bf16[96,1536]{1,0:T(8,128)(2,1)} async-done(((bf16[768,1536]{1,0:T(8,128)(2,1)}), bf16[96,1536]{1,0:T(8,128)(2,1)}) %reduce-scatter.9.cloned.1.call-update) | async-done | bytes 294928 | tf_op jit(solution)/shard_map/reduce_scatter | solution.py:97
  422.0 1.8 convert_element_type.52
  (7 shorter events, 0.1 us)
Async XLA Ops:
  7.2 164.6 %copy-start = (bf16[1,2,256,1536]{3,2,1,0:T(8,128)(2,1)S(1)}, bf16[1,2,256,1536]{3,2,1,0:T(8,128)(2,1)}, u32[]{:S(2)}) copy-start(bf16[1,2,256,1536]{3,2,1,0:T(8,128)(2,1)} %param.21) | copy-start | bytes 4718596
  7.2 11.0 %copy-start.7 = (s32[8]{0:T(128)S(1)}, s32[8]{0:T(128)}, u32[]{:S(2)}) copy-start(s32[8]{0:T(128)} %param.16) | copy-start | bytes 100
  7.2 13.6 %copy-start.3 = (bf16[384,64]{0,1:T(8,128)(2,1)S(1)}, bf16[384,64]{0,1:T(8,128)(2,1)}, u32[]{:S(2)}) copy-start(bf16[384,64]{0,1:T(8,128)(2,1)} %param.17) | copy-start | bytes 147460
  7.2 164.6 %all-gather.2.cloned.1.call-start = ((), (), s32[]{:S(2)}) async-start(), calls=%async_computation.4 | async-start | bytes 10616832 | tf_op jit(solution)/shard_map/all_gather | solution.py:56
  7.9 196.8 %reduce-scatter.11.cloned.1.call-start = ((), (), s32[]{:S(2)}) async-start(), calls=%async_computation.7 | async-start | bytes 491520 | tf_op jit(solution)/shard_map/reduce_scatter | solution.py:92
  14.5 45.1 %collective-permute-start = (bf16[8,2,128,512]{3,2,1,0:T(8,128)(2,1)}, bf16[8,2,128,512]{3,2,1,0:T(8,128)(2,1)}, u32[]{:S(2)}, u32[]{:S(2)}) collective-permute-start(bf16[8,2,128,512]{3,2,1,0:T(8,128)(2,1)} %fusion.3), channel_id=1, source_target_pairs={{0,8},{8,16},{16,24},{1,9},{9,17},{17,25},{2,10},{10,18},{18,26},{... | collective-permute-start | bytes 6291464 | tf_op jit(solution)/shard_map/ppermute | solution.py:10
  54.6 5.0 %copy-start.4 = (f32[1,3072]{1,0:T(1,128)S(1)}, f32[1,3072]{1,0:T(1,128)}, u32[]{:S(2)}) copy-start(f32[1,3072]{1,0:T(1,128)} %param.19) | copy-start | bytes 36868
  59.6 4.9 %copy-start.5 = (bf16[512,16]{0,1:T(8,128)(2,1)S(1)}, bf16[512,16]{0,1:T(8,128)(2,1)}, u32[]{:S(2)}) copy-start(bf16[512,16]{0,1:T(8,128)(2,1)} %param.14) | copy-start | bytes 49156
  111.7 2.6 copy-start.1
  171.8 10.6 %copy-start.2 = (f32[512,3072]{1,0:T(8,128)S(1)}, f32[512,3072]{1,0:T(8,128)}, u32[]{:S(2)}) copy-start(f32[512,3072]{1,0:T(8,128)} %copy-done.1) | copy-start | bytes 18874372
  182.3 2.9 copy-start.6
  185.2 100.7 %reduce-scatter.7.cloned.1.call-start = ((), (), s32[]{:S(2)}) async-start(), calls=%async_computation.5 | async-start | bytes 11796480 | tf_op jit(solution)/shard_map/reduce_scatter | solution.py:89
  196.4 154.2 %reduce-scatter.13.cloned.1.call-start = ((), (), s32[]{:S(2)}) async-start(), calls=%async_computation.8 | async-start | bytes 221184
  206.5 215.5 %reduce-scatter.9.cloned.1.call-start = ((), (), s32[]{:S(2)}) async-start(), calls=%async_computation.6 | async-start | bytes 2654208 | tf_op jit(solution)/shard_map/reduce_scatter | solution.py:97
Sparse Core Ops, SparseCore 0:
  10.2 161.4 all-gather.1
  185.3 19.4 reduce-scatter.10
  207.4 78.4 reduce-scatter.6
  289.5 61.0 reduce-scatter.12
  354.0 68.0 reduce-scatter.8
where the time goes:
time: 431 us; the launch traced here: 430 us
  waiting for transfers between devices  269 us (62%)
  blocking collectives  72.1 us (17%)
  matrix products  53.8 us (12%)
  between operations  15.9 us (4%)
  other arithmetic  9.72 us (2%)
  local copies, waits for them, and re-layouts  6.3 us (1%)
    reduce_scatter x1, waiting for transfers between devices, local(): lax.psum_scatter(grad_w.astype(jnp.bfloat16), 'enc', scatter_dimension=0,...  79.3 us
    reduce_scatter x1, waiting for transfers between devices, local(): lax.psum_scatter(part_w.astype(jnp.bfloat16), 'fsdp', scatter_dimension=0...  69.9 us
    all_gather x1, waiting for transfers between devices, local(): lax.all_gather(value_weight, 'fsdp', axis=0, tiled=True)  56.7 us
    unnamed x6, waiting for transfers between devices  54.5 us
    all_gather x1, blocking collectives, local(): everything = lax.all_gather(latent, 'fsdp', axis=2, tiled=True)  38.3 us
    all_gather x1, blocking collectives, local(): lax.all_gather(embed_weight, 'fsdp', axis=0, tiled=True)  33.8 us
    dot_general x1, matrix products, local(): lax.dot_general(modulated, cot_rows, (((0,), (0,)), ((), ())), preferred_...  11.2 us
    dot_general x1, matrix products, local(): jnp.dot(modulated, weight_full, preferred_element_type=jnp.float32)  11 us
  transfers between devices with their start and end apart: 6, of which 5 were waited for; matrix products, arithmetic and copies ran while one was open for 12% of the time, Pallas kernels for 0%

commit v1 on v0

v1 whole, which is shorter than its diff:
```python
import functools

import jax
import jax.numpy as jnp
from jax import lax
from jax.experimental import pallas as pl
from jax.experimental.pallas import tpu as pltpu
from jax.sharding import PartitionSpec as P

MESH = pl.DeviceIdType.MESH
F32, BF16 = jnp.float32, jnp.bfloat16
HIGH = lax.Precision.HIGHEST
VMEM = pl.BlockSpec(memory_space=pltpu.VMEM)
TAIL = 16


def dot(a, b, dims=((1,), (0,)), precision=None):
    return lax.dot_general(a, b, (dims, ((), ())), preferred_element_type=F32, precision=precision)


def meet(axes):
    barrier = pltpu.get_barrier_semaphore()
    total = 0
    for axis in axes:
        me, size = lax.axis_index(axis), lax.axis_size(axis)
        for k in range(1, size):
            pl.semaphore_signal(barrier, inc=1, device_id={axis: lax.rem(me + k, size)}, device_id_type=MESH)
        total += size - 1
    pl.semaphore_wait(barrier, total)


def spread(axis, source, target, sems):
    me, size = lax.axis_index(axis), lax.axis_size(axis)
    copies = []
    for k in range(1, size):
        peer = lax.rem(me + k, size)
        copy = pltpu.make_async_remote_copy(
            src_ref=source(peer), dst_ref=target(me),
            send_sem=sems.at[0, k - 1], recv_sem=sems.at[1, k - 1],
            device_id={axis: peer}, device_id_type=MESH)
        copy.start()
        copies.append(copy)
    return copies


def wait_all(copies):
    for copy in copies:
        copy.wait()


def prep_kernel(n_e, n_f, depth, embed_t, embed, weight, mod, full, gram, mod_all, weight_rows, embed_rows,
                part, landed, quarter, gsend, gland, mod_sems, gram_sems, part_sems, full_sems, row_sems):
    e, f = lax.axis_index("enc"), lax.axis_index("fsdp")
    width = embed_t.shape[0]
    rows = weight.shape[0]
    cols = weight.shape[1] // n_e
    block = rows // n_e
    mine = pl.ds(pl.multiple_of(e * cols, 128), cols)
    meet(("enc", "fsdp"))
    mod_copies = spread("fsdp", lambda peer: mod.at[peer], lambda me: mod_all.at[me], mod_sems)
    flat = embed_t[...]
    square = dot(flat, flat, ((1,), (1,)))
    total = jnp.sum(flat.astype(F32), axis=1, keepdims=True)
    gsend[...] = jnp.concatenate([square, jnp.broadcast_to(total, (width, width))], axis=1)
    gram_copies = spread("fsdp", lambda peer: gsend, lambda me: gland.at[me], gram_sems)
    mod_all[f] = mod[f]
    gland[f] = gsend[...]
    wait_all(mod_copies)
    wait_all(gram_copies)
    both = jnp.sum(gland[...], axis=0) * (1.0 / depth)
    mean = both[:, width:]
    mean_row = jnp.sum(mean * (lax.broadcasted_iota(jnp.int32, mean.shape, 0)
                               == lax.broadcasted_iota(jnp.int32, mean.shape, 1)).astype(F32), axis=0, keepdims=True)
    gram[...] = jnp.concatenate([both[:, :width] - mean * mean_row, mean], axis=1)
    centred = flat.astype(F32) - mean[:, :1]
    own = weight[:, mine]
    row_id = lax.broadcasted_iota(jnp.int32, (TAIL, rows), 0)
    for s in range(n_f):
        scale = 1.0 + mod_all[s, 0:1, :]
        shift = mod_all[s, 1:2, :]
        tail = jnp.where(row_id == 0, scale, jnp.where(row_id == 1, shift, 0.0))
        left = jnp.concatenate([centred * scale, tail], axis=0).astype(BF16)
        part[s] = dot(left, own).astype(BF16)
    part_copies = spread("fsdp", lambda peer: part.at[peer], lambda me: landed.at[me], part_sems)
    landed[f] = part[f]
    for k in range(n_e):
        where = n_e * f + k
        target, slot = lax.rem(where, n_f), where // n_f
        there = pl.ds(pl.multiple_of(slot * block, 16), block)
        here = pl.ds(k * block, block)

        def pair(make, slot=slot, there=there, here=here):
            return (make(weight.at[here, mine], weight_rows.at[there, :], slot, 0),
                    make(embed.at[here, :], embed_rows.at[there, :], slot, 1))

        @pl.when(target != f)
        def _(k=k, target=target, pair=pair):
            for copy in pair(lambda src, dst, slot, which: pltpu.make_async_remote_copy(
                    src_ref=src, dst_ref=dst, send_sem=row_sems.at[0, which, k], recv_sem=row_sems.at[1, which, slot],
                    device_id={"fsdp": target}, device_id_type=MESH)):
                copy.start()

        @pl.when(target == f)
        def _(k=k, pair=pair):
            for copy in pair(lambda src, dst, slot, which: pltpu.make_async_copy(src, dst, row_sems.at[0, which, k])):
                copy.start()
                copy.wait()

    wait_all(part_copies)
    quarter[...] = jnp.sum(landed[...].astype(F32), axis=0).astype(BF16)
    full_copies = spread("enc", lambda peer: quarter, lambda me: full.at[me], full_sems)
    full[e] = quarter[...]
    for k in range(n_e):
        where = n_e * f + k
        target = lax.rem(where, n_f)

        @pl.when(target != f)
        def _(k=k, target=target):
            here = pl.ds(k * block, block)
            for src, dst, which in ((weight.at[here, mine], weight_rows.at[here, :], 0), (embed.at[here, :], embed_rows.at[here, :], 1)):
                pltpu.make_async_remote_copy(
                    src_ref=src, dst_ref=dst, send_sem=row_sems.at[0, which, k], recv_sem=row_sems.at[1, which, k],
                    device_id={"fsdp": target}, device_id_type=MESH).wait_send()

    for slot in range(n_e):
        origin = (n_f * slot + f) // n_e

        @pl.when(origin != f)
        def _(slot=slot, origin=origin):
            here = pl.ds(slot * block, block)
            for src, dst, which in ((weight.at[here, mine], weight_rows.at[here, :], 0), (embed.at[here, :], embed_rows.at[here, :], 1)):
                pltpu.make_async_remote_copy(
                    src_ref=src, dst_ref=dst, send_sem=row_sems.at[0, which, slot], recv_sem=row_sems.at[1, which, slot],
                    device_id={"fsdp": origin}, device_id_type=MESH).wait_recv()

    wait_all(full_copies)


def encode_kernel(frames, assign, start, first, now, past, gain, taps, out_kernel, patches):
    s = pl.program_id(0)
    clip_start = start[assign[s]]
    pixels = now.shape[2]
    gains = gain[0:1, :]

    def norm(frame, frame_id):
        value = frame.astype(F32)
        live = jnp.where((frame_id >= clip_start) & (frame_id >= 0), 1.0, 0.0)
        scaling = lax.rsqrt(jnp.mean(value * value, axis=-1, keepdims=True) + 1e-06) * live
        return (value * scaling * gains).astype(BF16)

    base = first[0]
    normed = [norm(past[0, past.shape[1] - 2 + i], base - 2 + i) for i in range(2)]
    normed += [norm(now[0, i], base + i) for i in range(frames)]
    row = lax.broadcasted_iota(jnp.int32, (pixels, 4 * 16), 0)
    col = lax.broadcasted_iota(jnp.int32, (pixels, 4 * 16), 1)
    keep = lax.rem(row, 4) == col // 16
    pick = (lax.broadcasted_iota(jnp.int32, (pixels // 4, pixels), 0)
            == lax.broadcasted_iota(jnp.int32, (pixels // 4, pixels), 1) // 4).astype(BF16)
    left = jnp.concatenate([jnp.concatenate(normed[i:i + 3], axis=1) for i in range(frames)], axis=0)
    convolved = dot(left, taps[...])
    activation = jnp.concatenate([now[0, i] for i in range(frames)], axis=0).astype(F32)
    stored = (activation + convolved / (1.0 + jnp.exp(-convolved))).astype(BF16)
    latent = dot(stored, out_kernel[...])
    found = []
    for i in range(frames):
        live = jnp.where(base + i >= clip_start, 1.0, 0.0)
        wide = jnp.where(keep, latent[i * pixels:(i + 1) * pixels] * live, 0.0).astype(BF16)
        found.append(dot(pick, wide))
    patches[0] = jnp.concatenate(found, axis=0).astype(BF16)


def token_kernel(n_e, n_f, frames, depth, lat, full, gram, cot, mod_all, weight_rows, embed_rows,
                 values, grad_value, grad_embed,
                 tokens, left, qsend, qland, qsum, qall, rsend, rland, rsum, rall, vsend, vland, gsend, gland,
                 lat_sems, q_sems, r_sems, qa_sems, ra_sems, v_sems, g_sems):
    e, f = lax.axis_index("enc"), lax.axis_index("fsdp")
    width = lat.shape[2]
    each = lat.shape[1] // frames
    cols = full.shape[2]
    block = grad_value.shape[0]
    slim = width // n_e
    rows = weight_rows.shape[0]
    meet(("enc", "fsdp"))
    lat_copies = spread("fsdp", lambda peer: lat.at[peer], lambda me: tokens.at[me], lat_sems)
    tokens[f] = lat[f]
    unit_id = (lax.broadcasted_iota(jnp.int32, (width, width), 0)
               == lax.broadcasted_iota(jnp.int32, (width, width), 1)).astype(BF16)
    mean = gram[:, width:width + 1]
    centred = dot(unit_id, embed_rows[...], ((1,), (1,))) - mean
    row_id = lax.broadcasted_iota(jnp.int32, (TAIL, rows), 0)
    for s in range(n_f):
        tail = jnp.where(row_id == 0, mod_all[s, 3:4, :], 0.0)
        left[s] = jnp.concatenate([centred * (1.0 + mod_all[s, 2:3, :]), tail], axis=0).astype(BF16)
    wait_all(lat_copies)
    came = tokens[...].astype(F32)
    flat = jnp.concatenate(
        [came[:, i * each:(i + 1) * each, :].reshape(n_f * each, width) for i in range(frames)], axis=0)
    low = flat.astype(BF16)
    var = jnp.sum(flat * dot(flat, gram[:, :width], precision=HIGH), axis=1, keepdims=True)
    inv_std = lax.rsqrt(jnp.maximum(var, 0.0) + 1e-06)
    scaled = flat * inv_std
    count = flat.shape[0]
    ones = (lax.broadcasted_iota(jnp.int32, (count, width), 1) == 0).astype(F32)
    wide = jnp.concatenate([scaled, ones], axis=1).astype(BF16)
    dots = jnp.zeros((count, 1), F32)
    for i in range(n_e):
        here = slice(i * cols, (i + 1) * cols)
        factor = full[i]
        product = dot(low, factor[:width]) * inv_std
        values[:, here] = (product + factor[width:width + TAIL].astype(F32)[1:2]).astype(BF16)
        cot_part = cot[:, here]
        dots += jnp.sum(product * cot_part.astype(F32), axis=1, keepdims=True)
        qsend[i] = dot(wide, cot_part, ((0,), (0,)))[:width + TAIL].astype(BF16)
    q_copies = spread("enc", lambda peer: qsend.at[peer], lambda me: qland.at[me], q_sems)
    weighted = scaled * (inv_std * dots * (1.0 / depth))
    pairs = dot(weighted.astype(BF16), low, ((0,), (0,)))
    pairs = jnp.concatenate([pairs, jnp.zeros((width, width), F32)], axis=1)
    for i in range(n_e):
        rsend[i] = pairs[i * slim:(i + 1) * slim]
    r_copies = spread("enc", lambda peer: rsend.at[peer], lambda me: rland.at[me], r_sems)
    qland[e] = qsend[e]
    rland[e] = rsend[e]
    wait_all(q_copies)
    summed = jnp.sum(qland[...].astype(F32), axis=0)
    low_sum = summed.astype(BF16)
    qsum[...] = low_sum
    qall[f] = low_sum
    qa_copies = spread("fsdp", lambda peer: qsum, lambda me: qall.at[me], qa_sems)
    wait_all(r_copies)
    head = jnp.sum(rland[...], axis=0)
    ends = full[e][width:width + TAIL]
    drift = dot(ends, low_sum[:width], ((1,), (1,)))[:8] * (1.0 / depth)
    drift = jnp.where(lax.broadcasted_iota(jnp.int32, drift.shape, 0) == 0, drift, 0.0)
    both = jnp.concatenate([head, jnp.concatenate([drift, jnp.zeros_like(drift)], axis=1)], axis=0)
    rsum[...] = both
    rall[f] = both
    ra_copies = spread("fsdp", lambda peer: rsum, lambda me: rall.at[me], ra_sems)
    wait_all(qa_copies)
    every = qall[...].reshape(n_f * (width + TAIL), cols)
    lefts = left[...].reshape(n_f * (width + TAIL), rows)
    gradient = dot(lefts, every, ((0,), (0,)))
    for i in range(n_e):
        vsend[i] = gradient[i * block:(i + 1) * block].astype(BF16)
    v_copies = spread("enc", lambda peer: vsend.at[peer], lambda me: vland.at[me], v_sems)
    vland[e] = vsend[e]
    back = dot(every, weight_rows[...], ((1,), (1,)))
    total = jnp.zeros((width, rows), F32)
    for s in range(n_f):
        start = s * (width + TAIL)
        total += back[start:start + width] * (1.0 + mod_all[s, 2:3, :])
    wait_all(ra_copies)
    fix = jnp.sum(rall[...], axis=0)[:, :width]
    chosen = (lax.broadcasted_iota(jnp.int32, (slim + 8, width), 1)
              == lax.broadcasted_iota(jnp.int32, (slim + 8, width), 0) + e * slim) & (
                  lax.broadcasted_iota(jnp.int32, (slim + 8, width), 0) < slim)
    against = dot(chosen.astype(F32), centred, precision=HIGH)
    against = jnp.where(lax.broadcasted_iota(jnp.int32, against.shape, 0) == slim, 1.0, against)
    total -= dot(fix, against, ((0,), (0,)), precision=HIGH)
    turned = dot(total.astype(BF16), unit_id, ((0,), (0,)))
    turned = jnp.concatenate([turned, jnp.zeros_like(turned)], axis=1).astype(BF16)
    for i in range(n_e):
        gsend[i] = turned[i * block:(i + 1) * block]
    g_copies = spread("enc", lambda peer: gsend.at[peer], lambda me: gland.at[me], g_sems)
    gland[e] = gsend[e]
    wait_all(v_copies)
    for i in range(n_e):
        grad_value[:, i * cols:(i + 1) * cols] = vland[i].astype(F32)
    wait_all(g_copies)
    grad_embed[...] = jnp.sum(gland[...].astype(F32), axis=0)[:, :width]


def local(
    n_e,
    n_f,
    enc_features,
    enc_gain,
    enc_kernel,
    out_kernel,
    clip_start,
    assign,
    embed_weight,
    mod_shift,
    mod_scale,
    value_weight,
    value_cotangent,
):
    clips, frames, pixels, channels = enc_features.shape
    rows, half = value_weight.shape
    width = embed_weight.shape[1]
    depth, cols, block = rows * n_f, half // n_e, rows // n_e
    size = width + TAIL
    tokens = frames * value_cotangent.shape[2]
    shape = jax.ShapeDtypeStruct
    dma = lambda *n: pltpu.SemaphoreType.DMA(n)
    big = 56 * 1024 * 1024

    past = lax.ppermute(enc_features[:, frames - 2:], "enc", [(i, i + 1) for i in range(n_e - 1)])

    by_rows = lambda m: m.reshape(n_f, 1, rows)
    by_block = lambda m: m.reshape(n_e, n_f, block).transpose(1, 0, 2).reshape(n_f, 1, rows)
    mod = jnp.concatenate([by_rows(mod_scale), by_rows(mod_shift), by_block(mod_scale), by_block(mod_shift)], axis=1)
    full, gram, mod_all, weight_rows, embed_rows = pl.pallas_call(
        functools.partial(prep_kernel, n_e, n_f, depth),
        out_shape=(shape((n_e, size, cols), BF16), shape((width, 2 * width), F32), shape((n_f, 4, rows), F32),
                   shape((rows, cols), BF16), shape((rows, width), BF16)),
        in_specs=[VMEM] * 4, out_specs=(VMEM,) * 5,
        scratch_shapes=[
            pltpu.VMEM((n_f, size, cols), BF16), pltpu.VMEM((n_f, size, cols), BF16), pltpu.VMEM((size, cols), BF16),
            pltpu.VMEM((width, 2 * width), F32), pltpu.VMEM((n_f, width, 2 * width), F32),
            dma(2, n_f - 1), dma(2, n_f - 1), dma(2, n_f - 1), dma(2, n_e - 1), dma(2, 2, n_e)],
        compiler_params=pltpu.CompilerParams(collective_id=0, has_side_effects=True, vmem_limit_bytes=big),
        name="prepare",
    )(embed_weight.T, embed_weight, value_weight, mod)

    first = (lax.axis_index("enc") * frames).astype(jnp.int32).reshape(1)
    taps = enc_kernel.reshape(3 * channels, channels)
    spec = lambda shape, fn: pl.BlockSpec(shape, fn)
    fixed = lambda *shape: pl.BlockSpec(shape, lambda s, *_: (0,) * len(shape))
    lat = pl.pallas_call(
        functools.partial(encode_kernel, frames),
        out_shape=shape((clips, frames * pixels // 4, width), BF16),
        grid_spec=pltpu.PrefetchScalarGridSpec(
            num_scalar_prefetch=3, grid=(clips,),
            in_specs=[
                spec((1, frames, pixels, channels), lambda s, a, *_: (a[s], 0, 0, 0)),
                spec((1, 2, pixels, channels), lambda s, a, *_: (a[s], 0, 0, 0)),
                fixed(1, channels), fixed(3 * channels, channels), fixed(channels, width)],
            out_specs=spec((1, frames * pixels // 4, width), lambda s, *_: (s, 0, 0))),
        compiler_params=pltpu.CompilerParams(vmem_limit_bytes=big),
        name="encode",
    )(assign, clip_start, first, enc_features, past, enc_gain, taps, jnp.tile(out_kernel, (1, 4)))

    values, grad_value, grad_embed = pl.pallas_call(
        functools.partial(token_kernel, n_e, n_f, frames, depth),
        out_shape=(shape((tokens, half), BF16), shape((block, half), F32), shape((block, width), F32)),
        in_specs=[VMEM] * 7, out_specs=(VMEM,) * 3,
        scratch_shapes=[
            pltpu.VMEM((n_f, lat.shape[1], width), BF16), pltpu.VMEM((n_f, size, rows), BF16),
            pltpu.VMEM((n_e, size, cols), BF16), pltpu.VMEM((n_e, size, cols), BF16),
            pltpu.VMEM((size, cols), BF16), pltpu.VMEM((n_f, size, cols), BF16),
            pltpu.VMEM((n_e, width // n_e, 2 * width), F32), pltpu.VMEM((n_e, width // n_e, 2 * width), F32),
            pltpu.VMEM((width // n_e + 8, 2 * width), F32), pltpu.VMEM((n_f, width // n_e + 8, 2 * width), F32),
            pltpu.VMEM((n_e, block, cols), BF16), pltpu.VMEM((n_e, block, cols), BF16),
            pltpu.VMEM((n_e, block, 2 * width), BF16), pltpu.VMEM((n_e, block, 2 * width), BF16),
            dma(2, n_f - 1), dma(2, n_e - 1), dma(2, n_e - 1), dma(2, n_f - 1), dma(2, n_f - 1),
            dma(2, n_e - 1), dma(2, n_e - 1)],
        compiler_params=pltpu.CompilerParams(collective_id=1, has_side_effects=True, vmem_limit_bytes=big),
        name="tokens",
    )(lat, full, gram, value_cotangent.reshape(tokens, half), mod_all, weight_rows, embed_rows)
    return (values.reshape(value_cotangent.shape), grad_value, grad_embed)


def solution(mesh):
    in_specs = (
        P(None, "enc", "fsdp", None),
        P(),
        P(),
        P(),
        P(),
        P(),
        P("fsdp", None),
        P("fsdp", None),
        P("fsdp", None),
        P("fsdp", None),
        P("fsdp", "enc", None, None),
    )
    out_specs = (P("fsdp", "enc", None, None), P(("enc", "fsdp"), None), P(("enc", "fsdp"), None))
    body = functools.partial(local, mesh.shape["enc"], mesh.shape["fsdp"])
    return jax.shard_map(body, mesh=mesh, in_specs=in_specs, out_specs=out_specs, check_vma=False)
```

time: 431 us -> 110 us (0.26)
  waiting for transfers between devices: 269 us -> 0.01 us
  Pallas kernels: 0 us -> 92 us
  blocking collectives: 72.1 us -> 0 us
  matrix products: 53.8 us -> 0 us
  between operations: 15.9 us -> 0.7 us
  other arithmetic: 9.72 us -> 4.16 us
    reduce_scatter x3 -> x0, waiting for transfers between devices: 158 us -> none  [the longest x1 79.3 us: local(): lax.psum_scatter(grad_w.astype(jnp.bfloat16), 'enc', scatter_dimension=0,...]
    pallas_call x0 -> x3, Pallas kernels: none -> 92 us  [the longest x1 41.4 us: local(): pl.pallas_call(functools.partial(token_kernel, n_e, n_f, frames, depth),...]
    all_gather x2 -> x0, blocking collectives: 72.1 us -> none  [the longest x1 38.3 us: local(): everything = lax.all_gather(latent, 'fsdp', axis=2, tiled=True)]
    all_gather x1 -> x0, waiting for transfers between devices: 56.7 us -> none  [local(): lax.all_gather(value_weight, 'fsdp', axis=0, tiled=True)]
    unnamed x6 -> x0, waiting for transfers between devices: 54.5 us -> none
    dot_general x8 -> x0, matrix products: 53.8 us -> none  [the longest x1 11.2 us: local(): lax.dot_general(modulated, cot_rows, (((0,), (0,)), ((), ())), preferred_...]
    convert_element_type x4 -> x0, other arithmetic: 6.84 us -> none  [the longest x1 3.66 us: local(): (live_mask * channel_norm(activation, enc_gain[0])).astype(jnp.bfloat16)]
  transfers between devices with their start and end apart: 6 -> 1, of which waited for: 5 -> 0; matrix products, arithmetic and copies ran while one was open for 12% -> 7% of each run, Pallas kernels for 0% -> 36%
where the time goes in v1:
time: 110 us
  Pallas kernels  92 us (84%)
  local copies, waits for them, and re-layouts  10.3 us (9%)
  other arithmetic  4.16 us (4%)
  starting transfers between devices  2.49 us (2%)
    pallas_call x1, Pallas kernels, local(): pl.pallas_call(functools.partial(token_kernel, n_e, n_f, frames, depth),...  41.4 us
    pallas_call x1, Pallas kernels, local(): pl.pallas_call(functools.partial(prep_kernel, n_e, n_f, depth), out_shape...  39.6 us
    pallas_call x1, Pallas kernels, local(): pl.pallas_call(functools.partial(encode_kernel, frames), out_shape=shape(...  11 us
    unnamed x9, local copies, waits for them, and re-layouts  8.43 us
    unnamed x2, other arithmetic  2.77 us
    ppermute x1, starting transfers between devices, local(): lax.ppermute(enc_features[:, frames - 2:], 'enc', [(i, i + 1) for i in ra...  2.49 us
  transfers between devices with their start and end apart: 1, of which 0 were waited for; matrix products, arithmetic and copies ran while one was open for 7% of the time, Pallas kernels for 36%

profile of v1, /device:TPU:0, one launch (start us, length us, event | category | flops | bytes accessed | tf_op | source)
XLA Modules:
  0.0 109.6 jit_solution(5843538279707024005)
XLA Ops:
  0.6 2.5 %collective-permute-start = (bf16[8,2,128,512]{3,2,1,0:T(8,128)(2,1)}, bf16[8,2,128,512]{3,2,1,0:T(8,128)(2,1)S(1)}, u32[]{:S(2)}, u32[]{:S(2)}) collective-permute-start(bf16[8,2,128,512]{3,2,1,0:T(8,128)(2,1)} %now.1), channel_id=1, source_target_pairs={{0,8},{8,16},{16,24},{1,9},{9,17},{17,25},{2,10},{10,18},{18,26},{... | collective-permute-start | bytes 6291464 | tf_op jit(solution)/shard_map/ppermute | solution.py:297
  3.1 0.5 broadcast.9
  3.6 1.4 %reduce.6 = f32[3072]{0:T(1024)S(1)} reduce(f32[1,3072]{1,0:T(1,128)} %param.18, f32[]{:T(128)} %broadcast.9), dimensions={0}, to_apply=%param.18.reduce_sub_computation.3 | reduce | bytes 24580 | tf_op args[7]
  5.0 0.1 reshape.46
  5.1 0.1 reshape.47
  5.2 1.4 %reduce.7 = f32[3072]{0:T(1024)S(1)} reduce(f32[1,3072]{1,0:T(1,128)} %param.19, f32[]{:T(128)} %broadcast.9), dimensions={0}, to_apply=%param.19.reduce_sub_computation.3 | reduce | bytes 24580 | tf_op args[8]
  6.6 0.1 reshape.44
  6.7 0.1 reshape.45
  6.8 0.7 tile.4
  7.5 0.8 copy.19.out_kernel
  8.3 1.5 %copy.22.embed = bf16[384,64]{1,0:T(8,128)(2,1)} copy(bf16[384,64]{0,1:T(8,128)(2,1)} %param.17) | data formatting | bytes 98304 | tf_op args[6]
  9.8 1.4 %pad_maximum_fusion.mod = f32[8,4,384]{2,1,0:T(4,128)} fusion(f32[8,1,384]{2,1,0:T(1,128)S(1)} %reshape.47, f32[8,1,384]{2,1,0:T(1,128)S(1)} %reshape.45, f32[8,1,384]{2,1,0:T(1,128)} %bitcast.21, f32[8,1,384]{2,1,0:T(1,128)} %bitcast.22), kind=kLoop, calls=%fused_computation | loop fusion | flops 36864 | bytes 98304 | tf_op jit(solution)/shard_map/concatenate | solution.py:301
  11.2 39.6 %prepare.1 = (bf16[4,80,384]{2,1,0:T(8,128)(2,1)}, f32[64,128]{1,0:T(8,128)}, f32[8,4,384]{2,1,0:T(4,128)}, bf16[384,384]{1,0:T(8,128)(2,1)}, bf16[384,64]{1,0:T(8,128)(2,1)}) custom-call(bf16[64,384]{1,0:T(8,128)(2,1)} %bitcast.18, bf16[384,64]{1,0:T(8,128)(2,1)} %copy.22.embed, bf16[384,1536]{1,0:T(8,128)(2,1)} %weight.1, f32[8,4,384]{2,1,0:T(4,128)} %pad_maximum_fusion.mod), custom_call_target="tpu_custom_call" | custom-call | tf_op jit(solution)/shard_map/prepare/pallas_call | solution.py:302
  50.8 0.0 collective-permute-done.past
  50.8 0.0 copy-start
  50.8 1.3 %copy-done = bf16[8,2,128,512]{3,2,1,0:T(8,128)(2,1)} copy-done((bf16[8,2,128,512]{3,2,1,0:T(8,128)(2,1)}, bf16[8,2,128,512]{3,2,1,0:T(8,128)(2,1)S(1)}, u32[]{:S(2)}) %copy-start) | copy-done | bytes 2097176
  52.2 11.0 %encode.1.lat = bf16[8,64,64]{2,1,0:T(8,128)(2,1)} custom-call(s32[8]{0:T(128)} %assign.1, s32[8]{0:T(128)} %start.1, s32[1]{0:T(128)} %bitcast.first, bf16[8,2,128,512]{3,2,1,0:T(8,128)(2,1)} %now.1, bf16[8,2,128,512]{3,2,1,0:T(8,128)(2,1)} %copy-done, f32[1,512]{1,0:T(1,128)} %gain.1, bf16[1536,512]{1,0:T(8,128)(2,1)} %bitcast.16, ...), custom_call_target="tpu_custom_call" | custom-call | tf_op jit(solution)/shard_map/encode/pallas_call | solution.py:319
  63.1 41.4 %tokens.1 = (bf16[512,1536]{1,0:T(8,128)(2,1)}, f32[96,1536]{1,0:T(8,128)}, f32[96,64]{1,0:T(8,128)}) custom-call(bf16[8,64,64]{2,1,0:T(8,128)(2,1)} %encode.1.lat, bf16[4,80,384]{2,1,0:T(8,128)(2,1)} %get-tuple-element.11.full, f32[64,128]{1,0:T(8,128)} %get-tuple-element.12.gram, bf16[512,1536]{1,0:T(8,128)(2,1)} %bitcast.14, ...), custom_call_target="tpu_custom_call" | custom-call | tf_op jit(solution)/shard_map/tokens/pallas_call | solution.py:333
  104.6 1.5 %copy.23 = f32[96,64]{0,1:T(8,128)} copy(f32[96,64]{1,0:T(8,128)} %get-tuple-element.24) | data formatting | bytes 49152
  106.1 0.0 copy-start.1
  106.1 2.7 %copy.30 = bf16[1,2,256,1536]{3,2,1,0:T(8,128)(2,1)} copy(bf16[1,2,256,1536]{3,2,1,0:T(8,128)(2,1)} %bitcast.15) | data formatting | bytes 3145728
  108.8 0.0 copy-done.1
  108.8 0.8 copy.31
  (2 shorter events, 0.0 us)
Async XLA Ops:
  0.6 50.2 %collective-permute-start = (bf16[8,2,128,512]{3,2,1,0:T(8,128)(2,1)}, bf16[8,2,128,512]{3,2,1,0:T(8,128)(2,1)S(1)}, u32[]{:S(2)}, u32[]{:S(2)}) collective-permute-start(bf16[8,2,128,512]{3,2,1,0:T(8,128)(2,1)} %now.1), channel_id=1, source_target_pairs={{0,8},{8,16},{16,24},{1,9},{9,17},{17,25},{2,10},{10,18},{18,26},{... | collective-permute-start | bytes 6291464 | tf_op jit(solution)/shard_map/ppermute | solution.py:297
  50.8 1.4 %copy-start = (bf16[8,2,128,512]{3,2,1,0:T(8,128)(2,1)}, bf16[8,2,128,512]{3,2,1,0:T(8,128)(2,1)S(1)}, u32[]{:S(2)}) copy-start(bf16[8,2,128,512]{3,2,1,0:T(8,128)(2,1)S(1)} %collective-permute-done.past) | copy-start | bytes 6291460
  106.1 2.7 %copy-start.1 = (f32[96,1536]{1,0:T(8,128)S(1)}, f32[96,1536]{1,0:T(8,128)}, u32[]{:S(2)}) copy-start(f32[96,1536]{1,0:T(8,128)} %get-tuple-element.29) | copy-start | bytes 1769476

commit v2 on v1

v2 whole, which is shorter than its diff:
```python
import functools

import jax
import jax.numpy as jnp
from jax import lax
from jax.experimental import pallas as pl
from jax.experimental.pallas import tpu as pltpu
from jax.sharding import PartitionSpec as P

MESH = pl.DeviceIdType.MESH
F32, BF16 = jnp.float32, jnp.bfloat16
HIGH = lax.Precision.HIGHEST
VMEM = pl.BlockSpec(memory_space=pltpu.VMEM)
TAIL = 16


def dot(a, b, dims=((1,), (0,)), precision=None):
    return lax.dot_general(a, b, (dims, ((), ())), preferred_element_type=F32, precision=precision)


def meet(axes):
    barrier = pltpu.get_barrier_semaphore()
    total = 0
    for axis in axes:
        me, size = lax.axis_index(axis), lax.axis_size(axis)
        for k in range(1, size):
            pl.semaphore_signal(barrier, inc=1, device_id={axis: lax.rem(me + k, size)}, device_id_type=MESH)
        total += size - 1
    pl.semaphore_wait(barrier, total)


def spread(axis, source, target, sems):
    me, size = lax.axis_index(axis), lax.axis_size(axis)
    copies = []
    for k in range(1, size):
        peer = lax.rem(me + k, size)
        copy = pltpu.make_async_remote_copy(
            src_ref=source(peer), dst_ref=target(me),
            send_sem=sems.at[0, k - 1], recv_sem=sems.at[1, k - 1],
            device_id={axis: peer}, device_id_type=MESH)
        copy.start()
        copies.append(copy)
    return copies


def wait_all(copies):
    for copy in copies:
        copy.wait()


def program_kernel(n_e, n_f, frames, depth, start, assign, feat_hbm, gain, taps_hbm, out_t, embed_t, scale_row, shift_row,
                   weight, cot_hbm, values, grad_value, grad_embed,
                   feat, past, taps, own, cot, found, lat, tokens,
                   mod, mod_all, gsum, gram_all, part, landed, quarter, full, rows_out, rows_in, weight_rows,
                   left, staged, qsend, qland, qsum, qall, rsend, rland, rsum, rall, vsend, vland, gsend, gland,
                   load_sems, out_sems, halo_sems, mod_sems, gram_sems, part_sems, full_sems, row_sems,
                   lat_sems, q_sems, r_sems, qa_sems, ra_sems, v_sems, g_sems):
    e, f = lax.axis_index("enc"), lax.axis_index("fsdp")
    clips, _, pixels, channels = feat.shape
    width, rows = embed_t.shape
    cols = own.shape[2]
    block = rows // n_e
    slim = width // n_e
    each = pixels // 4
    mine = pl.ds(pl.multiple_of(e * cols, 128), cols)
    loads = [pltpu.make_async_copy(src, dst, load_sems.at[i]) for i, (src, dst) in enumerate(
        [(weight.at[:, :, mine], own), (feat_hbm, feat), (taps_hbm, taps), (cot_hbm, cot)])]
    for copy in loads:
        copy.start()
    for s in range(n_f):
        here = slice(s * rows, (s + 1) * rows)
        mod[s] = jnp.concatenate([scale_row[:, here], shift_row[:, here]], axis=0)
    flat = embed_t[...]
    square = dot(flat, flat, ((1,), (1,)))
    total = jnp.sum(flat.astype(F32), axis=1, keepdims=True)
    gsum[...] = jnp.concatenate([square, jnp.broadcast_to(total, (width, width))], axis=1)
    meet(("enc", "fsdp"))

    def halo(c, peer):
        return pltpu.make_async_remote_copy(
            src_ref=feat_hbm.at[c, pl.ds(frames - 2, 2)], dst_ref=past.at[c],
            send_sem=halo_sems.at[0, c], recv_sem=halo_sems.at[1, c],
            device_id={"enc": lax.rem(peer, n_e)}, device_id_type=MESH)

    mod_copies = spread("fsdp", lambda peer: mod.at[peer], lambda me: mod_all.at[me], mod_sems)
    gram_copies = spread("fsdp", lambda peer: gsum, lambda me: gram_all.at[me], gram_sems)

    @pl.when(e < n_e - 1)
    def _():
        @pl.loop(0, clips)
        def _(c):
            halo(c, e + 1).start()

    @pl.when(e == 0)
    def _():
        past[...] = jnp.zeros_like(past)

    def row_target(k):
        where = n_e * f + k
        return lax.rem(where, n_f), where // n_f

    def row_copy(which, k, slot, target=None):
        src = rows_out.at[k] if which else weight.at[k, :, mine]
        dst = (rows_in if which else weight_rows).at[slot]
        if target is None:
            return pltpu.make_async_copy(src, dst, row_sems.at[0, which, k])
        return pltpu.make_async_remote_copy(
            src_ref=src, dst_ref=dst, send_sem=row_sems.at[0, which, k], recv_sem=row_sems.at[1, which, slot],
            device_id={"fsdp": target}, device_id_type=MESH)

    def send_rows(which):
        for k in range(n_e):
            target, slot = row_target(k)

            @pl.when(target != f)
            def _(k=k, target=target, slot=slot):
                row_copy(which, k, slot, target).start()

            @pl.when(target == f)
            def _(k=k, target=target, slot=slot):
                inside = row_copy(which, k, slot)
                inside.start()
                inside.wait()

    send_rows(0)
    mod_all[f] = mod[f]
    gram_all[f] = gsum[...]
    wait_all(mod_copies)
    wait_all(gram_copies)
    both = jnp.sum(gram_all[...], axis=0) * (1.0 / depth)
    mean = both[:, width:]
    diagonal = (lax.broadcasted_iota(jnp.int32, mean.shape, 0) == lax.broadcasted_iota(jnp.int32, mean.shape, 1))
    gram = both[:, :width] - mean * jnp.sum(mean * diagonal.astype(F32), axis=0, keepdims=True)
    mean = mean[:, :1]
    unit_id = diagonal.astype(BF16)
    centred = flat.astype(F32) - mean
    loads[0].wait()
    own_flat = own[...].astype(F32).reshape(rows, cols).astype(BF16)
    row_id = lax.broadcasted_iota(jnp.int32, (TAIL, rows), 0)
    for s in range(n_f):
        scale = 1.0 + mod_all[s, 0:1, :]
        tail = jnp.where(row_id == 0, scale, jnp.where(row_id == 1, mod_all[s, 1:2, :], 0.0))
        factor = jnp.concatenate([centred * scale, tail], axis=0).astype(BF16)
        part[s] = dot(factor, own_flat).astype(BF16)
    part_copies = spread("fsdp", lambda peer: part.at[peer], lambda me: landed.at[me], part_sems)
    landed[f] = part[f]
    stack = [flat.astype(F32)] + [mod_all[s, 0:1, :] for s in range(n_f)] + [mod_all[s, 1:2, :] for s in range(n_f)]
    spare = rows_out.shape[2] - width - 2 * n_f
    if spare:
        stack.append(jnp.zeros((spare, rows), F32))
    rows_out[...] = jnp.concatenate(stack, axis=0).T.reshape(rows_out.shape)
    send_rows(1)

    gains = gain[0:1, :]
    base = e * frames
    row = lax.broadcasted_iota(jnp.int32, (pixels, width), 0)
    col = lax.broadcasted_iota(jnp.int32, (pixels, width), 1)
    keep = lax.rem(row, 4) == col // (width // 4)
    pick = (lax.broadcasted_iota(jnp.int32, (each, pixels), 0)
            == lax.broadcasted_iota(jnp.int32, (each, pixels), 1) // 4).astype(BF16)
    out_wide = jnp.concatenate([out_t[...]] * 4, axis=0)

    def encode(c, _):
        clip_start = start[c]

        @pl.when(e > 0)
        def _():
            halo(c, e + n_e - 1).wait_recv()

        def norm(frame, frame_id):
            value = frame.astype(F32)
            live = jnp.where((frame_id >= clip_start) & (frame_id >= 0), 1.0, 0.0)
            scaling = lax.rsqrt(jnp.mean(value * value, axis=-1, keepdims=True) + 1e-06) * live
            return (value * scaling * gains).astype(BF16)

        normed = [norm(past[c, i], base - 2 + i) for i in range(2)]
        normed += [norm(feat[c, i], base + i) for i in range(frames)]
        window = jnp.concatenate([jnp.concatenate(normed[i:i + 3], axis=1) for i in range(frames)], axis=0)
        convolved = dot(window, taps[...])
        activation = jnp.concatenate([feat[c, i] for i in range(frames)], axis=0).astype(F32)
        stored = (activation + convolved / (1.0 + jnp.exp(-convolved))).astype(BF16)
        latent = dot(stored, out_wide, ((1,), (1,)))
        picked = []
        for i in range(frames):
            live = jnp.where(base + i >= clip_start, 1.0, 0.0)
            picked.append(dot(pick, jnp.where(keep, latent[i * pixels:(i + 1) * pixels] * live, 0.0).astype(BF16)))
        found[c] = jnp.concatenate(picked, axis=0).astype(BF16)
        return 0

    loads[1].wait()
    loads[2].wait()
    cut = clips // 2
    lax.fori_loop(0, cut, encode, 0)
    wait_all(part_copies)
    quarter[...] = jnp.sum(landed[...].astype(F32), axis=0).astype(BF16)
    full_copies = spread("enc", lambda peer: quarter, lambda me: full.at[me], full_sems)
    full[e] = quarter[...]
    for which in range(2):
        for k in range(n_e):
            target, slot = row_target(k)

            @pl.when(target != f)
            def _(which=which, k=k, target=target, slot=slot):
                row_copy(which, k, slot, target).wait_send()

        for slot in range(n_e):
            origin = (n_f * slot + f) // n_e

            @pl.when(origin != f)
            def _(which=which, slot=slot, origin=origin):
                row_copy(which, slot, slot, origin).wait_recv()

    turned_in = rows_in[...].reshape(rows, rows_in.shape[2]).T
    weight_flat = weight_rows[...].astype(F32).reshape(rows, cols).astype(BF16)
    centred = turned_in[:width] - mean
    for s in range(n_f):
        tail = jnp.where(row_id == 0, turned_in[width + n_f + s:width + n_f + s + 1], 0.0)
        left[s] = jnp.concatenate([centred * (1.0 + turned_in[width + s:width + s + 1]), tail], axis=0).astype(BF16)
    lax.fori_loop(cut, clips, encode, 0)
    for s in range(n_f):
        lat[s] = found[assign[s]]
    lat_copies = spread("fsdp", lambda peer: lat.at[peer], lambda me: tokens.at[me], lat_sems)
    tokens[f] = lat[f]
    wait_all(full_copies)
    loads[3].wait()
    wait_all(lat_copies)
    came = tokens[...].astype(F32)
    flat = jnp.concatenate(
        [came[:, i * each:(i + 1) * each, :].reshape(n_f * each, width) for i in range(frames)], axis=0)
    low = flat.astype(BF16)
    var = jnp.sum(flat * dot(flat, gram, precision=HIGH), axis=1, keepdims=True)
    inv_std = lax.rsqrt(jnp.maximum(var, 0.0) + 1e-06)
    scaled = flat * inv_std
    count = flat.shape[0]
    ones = (lax.broadcasted_iota(jnp.int32, (count, width), 1) == 0).astype(F32)
    wide = jnp.concatenate([scaled, ones], axis=1).astype(BF16)
    dots = jnp.zeros((count, 1), F32)
    out_copies = []
    for i in range(n_e):
        here = slice(i * cols, (i + 1) * cols)
        factor = full[i]
        product = dot(low, factor[:width]) * inv_std
        staged[i] = (product + factor[width:width + TAIL].astype(F32)[1:2]).astype(BF16)
        out_copies.append(pltpu.make_async_copy(staged.at[i], values.at[:, pl.ds(i * cols, cols)], out_sems.at[i]))
        out_copies[-1].start()
        cot_part = cot[:, here]
        dots += jnp.sum(product * cot_part.astype(F32), axis=1, keepdims=True)
        qsend[i] = dot(wide, cot_part, ((0,), (0,)))[:width + TAIL].astype(BF16)
    q_copies = spread("enc", lambda peer: qsend.at[peer], lambda me: qland.at[me], q_sems)
    weighted = scaled * (inv_std * dots * (1.0 / depth))
    pairs = dot(weighted.astype(BF16), low, ((0,), (0,)))
    pairs = jnp.concatenate([pairs, jnp.zeros((width, width), F32)], axis=1)
    for i in range(n_e):
        rsend[i] = pairs[i * slim:(i + 1) * slim]
    r_copies = spread("enc", lambda peer: rsend.at[peer], lambda me: rland.at[me], r_sems)
    qland[e] = qsend[e]
    rland[e] = rsend[e]
    wait_all(q_copies)
    summed = jnp.sum(qland[...].astype(F32), axis=0)
    low_sum = summed.astype(BF16)
    qsum[...] = low_sum
    qall[f] = low_sum
    qa_copies = spread("fsdp", lambda peer: qsum, lambda me: qall.at[me], qa_sems)
    wait_all(r_copies)
    head = jnp.sum(rland[...], axis=0)
    ends = full[e][width:width + TAIL]
    drift = dot(ends, low_sum[:width], ((1,), (1,)))[:8] * (1.0 / depth)
    drift = jnp.where(lax.broadcasted_iota(jnp.int32, drift.shape, 0) == 0, drift, 0.0)
    both = jnp.concatenate([head, jnp.concatenate([drift, jnp.zeros_like(drift)], axis=1)], axis=0)
    rsum[...] = both
    rall[f] = both
    ra_copies = spread("fsdp", lambda peer: rsum, lambda me: rall.at[me], ra_sems)
    wait_all(qa_copies)
    every = qall[...].reshape(n_f * (width + TAIL), cols)
    lefts = left[...].reshape(n_f * (width + TAIL), rows)
    gradient = dot(lefts, every, ((0,), (0,)))
    for i in range(n_e):
        vsend[i] = gradient[i * block:(i + 1) * block].astype(BF16)
    v_copies = spread("enc", lambda peer: vsend.at[peer], lambda me: vland.at[me], v_sems)
    vland[e] = vsend[e]
    back = dot(every, weight_flat, ((1,), (1,)))
    total = jnp.zeros((width, rows), F32)
    for s in range(n_f):
        start = s * (width + TAIL)
        total += back[start:start + width] * (1.0 + turned_in[width + s:width + s + 1])
    wait_all(ra_copies)
    fix = jnp.sum(rall[...], axis=0)[:, :width]
    chosen = (lax.broadcasted_iota(jnp.int32, (slim + 8, width), 1)
              == lax.broadcasted_iota(jnp.int32, (slim + 8, width), 0) + e * slim) & (
                  lax.broadcasted_iota(jnp.int32, (slim + 8, width), 0) < slim)
    against = dot(chosen.astype(F32), centred, precision=HIGH)
    against = jnp.where(lax.broadcasted_iota(jnp.int32, against.shape, 0) == slim, 1.0, against)
    total -= dot(fix, against, ((0,), (0,)), precision=HIGH)
    turned = dot(total.astype(BF16), unit_id, ((0,), (0,)))
    turned = jnp.concatenate([turned, jnp.zeros_like(turned)], axis=1).astype(BF16)
    for i in range(n_e):
        gsend[i] = turned[i * block:(i + 1) * block]
    g_copies = spread("enc", lambda peer: gsend.at[peer], lambda me: gland.at[me], g_sems)
    gland[e] = gsend[e]
    wait_all(v_copies)
    for i in range(n_e):
        grad_value[:, i * cols:(i + 1) * cols] = vland[i].astype(F32)
    wait_all(g_copies)
    grad_embed[...] = jnp.sum(gland[...].astype(F32), axis=0)[:, :width]
    wait_all(out_copies)

    @pl.when(e < n_e - 1)
    def _():
        @pl.loop(0, clips)
        def _(c):
            halo(c, e + 1).wait_send()


def local(
    n_e,
    n_f,
    enc_features,
    enc_gain,
    enc_kernel,
    out_kernel,
    clip_start,
    assign,
    embed_weight,
    mod_shift,
    mod_scale,
    value_weight,
    value_cotangent,
):
    clips, frames, pixels, channels = enc_features.shape
    rows, half = value_weight.shape
    width = embed_weight.shape[1]
    depth, cols, block = rows * n_f, half // n_e, rows // n_e
    size = width + TAIL
    slim = width // n_e
    count = frames * value_cotangent.shape[2]
    lanes = -(-(width + 2 * n_f) // 128) * 128
    shape = jax.ShapeDtypeStruct
    dma = lambda *n: pltpu.SemaphoreType.DMA(n)
    b16 = lambda *n: pltpu.VMEM(n, BF16)
    f32 = lambda *n: pltpu.VMEM(n, F32)
    scalars = pl.BlockSpec(memory_space=pltpu.SMEM)
    far = pl.BlockSpec(memory_space=pl.ANY)
    patches = frames * pixels // 4
    values, grad_value, grad_embed = pl.pallas_call(
        functools.partial(program_kernel, n_e, n_f, frames, depth),
        out_shape=(shape((count, half), BF16), shape((block, half), F32), shape((block, width), F32)),
        in_specs=[scalars, scalars, far, VMEM, far, VMEM, VMEM, VMEM, VMEM, far, far],
        out_specs=(far, VMEM, VMEM),
        scratch_shapes=[
            b16(clips, frames, pixels, channels), b16(clips, 2, pixels, channels), b16(3 * channels, channels),
            b16(n_e, block, cols), b16(count, half), b16(clips, patches, width), b16(n_f, patches, width),
            b16(n_f, patches, width),
            f32(n_f, 2, rows), f32(n_f, 2, rows), f32(width, 2 * width), f32(n_f, width, 2 * width),
            b16(n_f, size, cols), b16(n_f, size, cols), b16(size, cols), b16(n_e, size, cols),
            f32(n_e, block, lanes), f32(n_e, block, lanes), b16(n_e, block, cols),
            b16(n_f, size, rows), b16(n_e, count, cols),
            b16(n_e, size, cols), b16(n_e, size, cols), b16(size, cols), b16(n_f, size, cols),
            f32(n_e, slim, 2 * width), f32(n_e, slim, 2 * width), f32(slim + 8, 2 * width), f32(n_f, slim + 8, 2 * width),
            b16(n_e, block, cols), b16(n_e, block, cols), b16(n_e, block, 2 * width), b16(n_e, block, 2 * width),
            dma(4), dma(n_e), dma(2, clips), dma(2, n_f - 1), dma(2, n_f - 1), dma(2, n_f - 1), dma(2, n_e - 1),
            dma(2, 2, n_e),
            dma(2, n_f - 1), dma(2, n_e - 1), dma(2, n_e - 1), dma(2, n_f - 1), dma(2, n_f - 1),
            dma(2, n_e - 1), dma(2, n_e - 1)],
        compiler_params=pltpu.CompilerParams(
            collective_id=0, has_side_effects=True, vmem_limit_bytes=56 * 1024 * 1024),
        name="program",
    )(clip_start, assign, enc_features, enc_gain, enc_kernel.reshape(3 * channels, channels), out_kernel.T,
      embed_weight.T, mod_scale, mod_shift, value_weight.reshape(n_e, block, half), value_cotangent.reshape(count, half))
    return (values.reshape(value_cotangent.shape), grad_value, grad_embed)


def solution(mesh):
    in_specs = (
        P(None, "enc", "fsdp", None),
        P(),
        P(),
        P(),
        P(),
        P(),
        P("fsdp", None),
        P("fsdp", None),
        P("fsdp", None),
        P("fsdp", None),
        P("fsdp", "enc", None, None),
    )
    out_specs = (P("fsdp", "enc", None, None), P(("enc", "fsdp"), None), P(("enc", "fsdp"), None))
    body = functools.partial(local, mesh.shape["enc"], mesh.shape["fsdp"])
    return jax.shard_map(body, mesh=mesh, in_specs=in_specs, out_specs=out_specs, check_vma=False)
```

time: 110 us -> 86.2 us (0.78)
  Pallas kernels: 92 us -> 80.3 us
  local copies, waits for them, and re-layouts: 10.3 us -> 5.03 us
  other arithmetic: 4.16 us -> 0 us
  starting transfers between devices: 2.49 us -> 0 us
    pallas_call x3 -> x1, Pallas kernels: 92 us -> 80.3 us  [local(): pl.pallas_call(functools.partial(program_kernel, n_e, n_f, frames, depth)...]
    unnamed x9 -> x5, local copies, waits for them, and re-layouts: 8.43 us -> 5.03 us
    unnamed x2 -> x0, other arithmetic: 2.77 us -> none
    ppermute x1 -> x0, starting transfers between devices: 2.49 us -> none  [local(): lax.ppermute(enc_features[:, frames - 2:], 'enc', [(i, i + 1) for i in ra...]
    another operation x2 -> x0, local copies, waits for them, and re-layouts: 1.49 us -> none  [local(): jnp.tile(out_kernel, (1, 4))]
    concatenate x1 -> x0, other arithmetic: 1.39 us -> none  [local(): jnp.concatenate([by_rows(mod_scale), by_rows(mod_shift), by_block(mod_sca...]
  transfers between devices with their start and end apart: 1 -> 0, of which waited for: 0 -> 0; matrix products, arithmetic and copies ran while one was open for 7% -> 0% of each run, Pallas kernels for 36% -> 0%
where the time goes in v2:
time: 86.2 us; the launch traced here: 85.9 us
  Pallas kernels  80.3 us (93%)
  local copies, waits for them, and re-layouts  5.03 us (6%)
    pallas_call x1, Pallas kernels, local(): pl.pallas_call(functools.partial(program_kernel, n_e, n_f, frames, depth)...  80.3 us
    unnamed x5, local copies, waits for them, and re-layouts  5.03 us

profile of v2, /device:TPU:0, one launch (start us, length us, event | category | flops | bytes accessed | tf_op | source)
XLA Modules:
  0.0 85.9 jit_solution(16878279254436277154)
XLA Ops:
  0.6 80.3 %program.1 = (bf16[512,1536]{1,0:T(8,128)(2,1)}, f32[96,1536]{1,0:T(8,128)}, f32[96,64]{1,0:T(8,128)}) custom-call(s32[8]{0:T(128)} %start.1, s32[8]{0:T(128)} %assign.1, bf16[8,2,128,512]{3,2,1,0:T(8,128)(2,1)} %feat_hbm.1, f32[1,512]{1,0:T(1,128)} %gain.1, bf16[1536,512]{1,0:T(8,128)(2,1)} %bitcast.7, bf16[16,512]{1,0:T(8,128)(2,1)} %bitcast.11, ...), custom_call_target="tpu_custom_call" | custom-call | tf_op jit(solution)/shard_map/program/pallas_call | solution.py:344
  80.9 1.5 %copy.14 = f32[96,64]{0,1:T(8,128)} copy(f32[96,64]{1,0:T(8,128)} %get-tuple-element.11) | data formatting | bytes 49152
  82.4 0.0 copy-start
  82.4 2.7 %copy.17 = bf16[1,2,256,1536]{3,2,1,0:T(8,128)(2,1)} copy(bf16[1,2,256,1536]{3,2,1,0:T(8,128)(2,1)} %bitcast.6) | data formatting | bytes 3145728
  85.1 0.0 copy-done
  85.1 0.8 copy.18
Async XLA Ops:
  82.4 2.7 %copy-start = (f32[96,1536]{1,0:T(8,128)S(1)}, f32[96,1536]{1,0:T(8,128)}, u32[]{:S(2)}) copy-start(f32[96,1536]{1,0:T(8,128)} %get-tuple-element.16) | copy-start | bytes 1769476

commit v3 on v2

--- a/solution.py
+++ b/solution.py
@@ -52,9 +52,9 @@
                    weight, cot_hbm, values, grad_value, grad_embed,
                    feat, past, taps, own, cot, found, lat, tokens,
                    mod, mod_all, gsum, gram_all, part, landed, quarter, full, rows_out, rows_in, weight_rows,
-                   left, staged, qsend, qland, qsum, qall, rsend, rland, rsum, rall, vsend, vland, gsend, gland,
+                   left, staged, qsend, qland, qsum, qall, rsend, rland, vsend, vland, gsend, gland,
                    load_sems, out_sems, halo_sems, mod_sems, gram_sems, part_sems, full_sems, row_sems,
-                   lat_sems, q_sems, r_sems, qa_sems, ra_sems, v_sems, g_sems):
+                   lat_sems, q_sems, r_sems, qa_sems, v_sems, g_sems):
     e, f = lax.axis_index("enc"), lax.axis_index("fsdp")
     clips, _, pixels, channels = feat.shape
     width, rows = embed_t.shape
@@ -236,41 +236,65 @@
     wide = jnp.concatenate([scaled, ones], axis=1).astype(BF16)
     dots = jnp.zeros((count, 1), F32)
     out_copies = []
-    for i in range(n_e):
-        here = slice(i * cols, (i + 1) * cols)
-        factor = full[i]
+    q_copies = []
+    for k in range(1, n_e + 1):
+        peer = lax.rem(e + k, n_e)
+        here = pl.ds(pl.multiple_of(peer * cols, 128), cols)
+        factor = full[peer]
+        cot_part = cot[:, here]
+        qsend[k - 1] = dot(wide, cot_part, ((0,), (0,)))[:width + TAIL].astype(BF16)
+        if k < n_e:
+            q_copies.append(pltpu.make_async_remote_copy(
+                src_ref=qsend.at[k - 1], dst_ref=qland.at[e],
+                send_sem=q_sems.at[0, k - 1], recv_sem=q_sems.at[1, k - 1],
+                device_id={"enc": peer}, device_id_type=MESH))
+            q_copies[-1].start()
         product = dot(low, factor[:width]) * inv_std
-        staged[i] = (product + factor[width:width + TAIL].astype(F32)[1:2]).astype(BF16)
-        out_copies.append(pltpu.make_async_copy(staged.at[i], values.at[:, pl.ds(i * cols, cols)], out_sems.at[i]))
+        staged[k - 1] = (product + factor[width:width + TAIL].astype(F32)[1:2]).astype(BF16)
+        out_copies.append(pltpu.make_async_copy(staged.at[k - 1], values.at[:, here], out_sems.at[k - 1]))
         out_copies[-1].start()
-        cot_part = cot[:, here]
         dots += jnp.sum(product * cot_part.astype(F32), axis=1, keepdims=True)
-        qsend[i] = dot(wide, cot_part, ((0,), (0,)))[:width + TAIL].astype(BF16)
-    q_copies = spread("enc", lambda peer: qsend.at[peer], lambda me: qland.at[me], q_sems)
     weighted = scaled * (inv_std * dots * (1.0 / depth))
     pairs = dot(weighted.astype(BF16), low, ((0,), (0,)))
     pairs = jnp.concatenate([pairs, jnp.zeros((width, width), F32)], axis=1)
     for i in range(n_e):
         rsend[i] = pairs[i * slim:(i + 1) * slim]
     r_copies = spread("enc", lambda peer: rsend.at[peer], lambda me: rland.at[me], r_sems)
-    qland[e] = qsend[e]
+    qland[e] = qsend[n_e - 1]
     rland[e] = rsend[e]
     wait_all(q_copies)
     summed = jnp.sum(qland[...].astype(F32), axis=0)
-    low_sum = summed.astype(BF16)
-    qsum[...] = low_sum
-    qall[f] = low_sum
-    qa_copies = spread("fsdp", lambda peer: qsum, lambda me: qall.at[me], qa_sems)
+    low_sum = summed[:width].astype(BF16)
+    ends = full[e][width:width + TAIL]
+    drift = dot(ends, low_sum, ((1,), (1,)))[:8] * (1.0 / depth)
+    drift = jnp.where(lax.broadcasted_iota(jnp.int32, drift.shape, 0) == 0, drift, 0.0)
     wait_all(r_copies)
     head = jnp.sum(rland[...], axis=0)
-    ends = full[e][width:width + TAIL]
-    drift = dot(ends, low_sum[:width], ((1,), (1,)))[:8] * (1.0 / depth)
-    drift = jnp.where(lax.broadcasted_iota(jnp.int32, drift.shape, 0) == 0, drift, 0.0)
-    both = jnp.concatenate([head, jnp.concatenate([drift, jnp.zeros_like(drift)], axis=1)], axis=0)
-    rsum[...] = both
-    rall[f] = both
-    ra_copies = spread("fsdp", lambda peer: rsum, lambda me: rall.at[me], ra_sems)
-    wait_all(qa_copies)
+    extra = [head[i:i + 8] for i in range(0, slim, 8)] + [jnp.concatenate([drift, jnp.zeros_like(drift)], axis=1)]
+    if cols > len(extra) * 2 * width:
+        extra.append(jnp.zeros((8, cols - len(extra) * 2 * width), F32))
+    mixed_sum = jnp.concatenate([summed[:width + 8], jnp.concatenate(extra, axis=1)], axis=0).astype(BF16)
+    qsum[...] = mixed_sum
+    half_ring = n_f // 2
+    partner = f + 1 - 2 * lax.rem(f, 2)
+
+    def onward(src, origin, peer, index):
+        copy = pltpu.make_async_remote_copy(
+            src_ref=src, dst_ref=qall.at[origin], send_sem=qa_sems.at[0, index], recv_sem=qa_sems.at[1, index],
+            device_id={"fsdp": peer}, device_id_type=MESH)
+        copy.start()
+        return copy
+
+    straight = [onward(qsum, f, lax.rem(f + 2 * j, n_f), j - 1) for j in range(1, half_ring)]
+    handed = [onward(qsum, f, partner, half_ring - 1)]
+    qall[f] = mixed_sum
+    for j in range(1, half_ring):
+        straight[j - 1].wait_recv()
+        origin = lax.rem(f + n_f - 2 * j, n_f)
+        handed.append(onward(qall.at[origin], origin, partner, half_ring - 1 + j))
+    for copy in straight:
+        copy.wait_send()
+    wait_all(handed)
     every = qall[...].reshape(n_f * (width + TAIL), cols)
     lefts = left[...].reshape(n_f * (width + TAIL), rows)
     gradient = dot(lefts, every, ((0,), (0,)))
@@ -283,8 +307,8 @@
     for s in range(n_f):
         start = s * (width + TAIL)
         total += back[start:start + width] * (1.0 + turned_in[width + s:width + s + 1])
-    wait_all(ra_copies)
-    fix = jnp.sum(rall[...], axis=0)[:, :width]
+    corner = sum(qall[s, width:width + TAIL].astype(F32)[8:] for s in range(n_f))
+    fix = jnp.concatenate([corner[:, i * 2 * width:i * 2 * width + width] for i in range(slim // 8 + 1)], axis=0)
     chosen = (lax.broadcasted_iota(jnp.int32, (slim + 8, width), 1)
               == lax.broadcasted_iota(jnp.int32, (slim + 8, width), 0) + e * slim) & (
                   lax.broadcasted_iota(jnp.int32, (slim + 8, width), 0) < slim)
@@ -355,11 +379,11 @@
             f32(n_e, block, lanes), f32(n_e, block, lanes), b16(n_e, block, cols),
             b16(n_f, size, rows), b16(n_e, count, cols),
             b16(n_e, size, cols), b16(n_e, size, cols), b16(size, cols), b16(n_f, size, cols),
-            f32(n_e, slim, 2 * width), f32(n_e, slim, 2 * width), f32(slim + 8, 2 * width), f32(n_f, slim + 8, 2 * width),
+            f32(n_e, slim, 2 * width), f32(n_e, slim, 2 * width),
             b16(n_e, block, cols), b16(n_e, block, cols), b16(n_e, block, 2 * width), b16(n_e, block, 2 * width),
             dma(4), dma(n_e), dma(2, clips), dma(2, n_f - 1), dma(2, n_f - 1), dma(2, n_f - 1), dma(2, n_e - 1),
             dma(2, 2, n_e),
-            dma(2, n_f - 1), dma(2, n_e - 1), dma(2, n_e - 1), dma(2, n_f - 1), dma(2, n_f - 1),
+            dma(2, n_f - 1), dma(2, n_e - 1), dma(2, n_e - 1), dma(2, n_f - 1),
             dma(2, n_e - 1), dma(2, n_e - 1)],
         compiler_params=pltpu.CompilerParams(
             collective_id=0, has_side_effects=True, vmem_limit_bytes=56 * 1024 * 1024),

time: 86.2 us -> 83.3 us (0.966)
  Pallas kernels: 80.3 us -> 77.3 us
    pallas_call x1, Pallas kernels: 80.3 us -> 77.3 us  [local(): pl.pallas_call(functools.partial(program_kernel, n_e, n_f, frames, depth)...]
where the time goes in v3:
time: 83.3 us; the launch traced here: 83 us
  Pallas kernels  77.3 us (93%)
  local copies, waits for them, and re-layouts  5.03 us (6%)
    pallas_call x1, Pallas kernels, local(): pl.pallas_call(functools.partial(program_kernel, n_e, n_f, frames, depth)...  77.3 us
    unnamed x5, local copies, waits for them, and re-layouts  5.03 us

profile of v3, /device:TPU:0, one launch (start us, length us, event | category | flops | bytes accessed | tf_op | source)
XLA Modules:
  0.0 83.0 jit_solution(17223108624863539239)
XLA Ops:
  0.6 77.3 %program.1 = (bf16[512,1536]{1,0:T(8,128)(2,1)}, f32[96,1536]{1,0:T(8,128)}, f32[96,64]{1,0:T(8,128)}) custom-call(s32[8]{0:T(128)} %start.1, s32[8]{0:T(128)} %assign.1, bf16[8,2,128,512]{3,2,1,0:T(8,128)(2,1)} %feat_hbm.1, f32[1,512]{1,0:T(1,128)} %gain.1, bf16[1536,512]{1,0:T(8,128)(2,1)} %bitcast.7, bf16[16,512]{1,0:T(8,128)(2,1)} %bitcast.11, ...), custom_call_target="tpu_custom_call" | custom-call | tf_op jit(solution)/shard_map/program/pallas_call | solution.py:368
  77.9 1.5 %copy.14 = f32[96,64]{0,1:T(8,128)} copy(f32[96,64]{1,0:T(8,128)} %get-tuple-element.11) | data formatting | bytes 49152
  79.4 0.0 copy-start
  79.4 2.7 %copy.17 = bf16[1,2,256,1536]{3,2,1,0:T(8,128)(2,1)} copy(bf16[1,2,256,1536]{3,2,1,0:T(8,128)(2,1)} %bitcast.6) | data formatting | bytes 3145728
  82.2 0.0 copy-done
  82.2 0.8 copy.18
Async XLA Ops:
  79.4 2.7 %copy-start = (f32[96,1536]{1,0:T(8,128)S(1)}, f32[96,1536]{1,0:T(8,128)}, u32[]{:S(2)}) copy-start(f32[96,1536]{1,0:T(8,128)} %get-tuple-element.16) | copy-start | bytes 1769476

commit v4 on v3

--- a/solution.py
+++ b/solution.py
@@ -26,7 +26,7 @@
         for k in range(1, size):
             pl.semaphore_signal(barrier, inc=1, device_id={axis: lax.rem(me + k, size)}, device_id_type=MESH)
         total += size - 1
-    pl.semaphore_wait(barrier, total)
+    return barrier, total
 
 
 def spread(axis, source, target, sems):
@@ -63,6 +63,7 @@
     slim = width // n_e
     each = pixels // 4
     mine = pl.ds(pl.multiple_of(e * cols, 128), cols)
+    barrier, arrivals = meet(("enc", "fsdp"))
     loads = [pltpu.make_async_copy(src, dst, load_sems.at[i]) for i, (src, dst) in enumerate(
         [(weight.at[:, :, mine], own), (feat_hbm, feat), (taps_hbm, taps), (cot_hbm, cot)])]
     for copy in loads:
@@ -74,7 +75,7 @@
     square = dot(flat, flat, ((1,), (1,)))
     total = jnp.sum(flat.astype(F32), axis=1, keepdims=True)
     gsum[...] = jnp.concatenate([square, jnp.broadcast_to(total, (width, width))], axis=1)
-    meet(("enc", "fsdp"))
+    pl.semaphore_wait(barrier, arrivals)
 
     def halo(c, peer):
         return pltpu.make_async_remote_copy(
@@ -325,7 +326,7 @@
     for i in range(n_e):
         grad_value[:, i * cols:(i + 1) * cols] = vland[i].astype(F32)
     wait_all(g_copies)
-    grad_embed[...] = jnp.sum(gland[...].astype(F32), axis=0)[:, :width]
+    grad_embed[...] = dot(diagonal.astype(F32), jnp.sum(gland[...].astype(F32), axis=0)[:, :width], ((1,), (1,)), HIGH)
     wait_all(out_copies)
 
     @pl.when(e < n_e - 1)
@@ -367,7 +368,7 @@
     patches = frames * pixels // 4
     values, grad_value, grad_embed = pl.pallas_call(
         functools.partial(program_kernel, n_e, n_f, frames, depth),
-        out_shape=(shape((count, half), BF16), shape((block, half), F32), shape((block, width), F32)),
+        out_shape=(shape((count, half), BF16), shape((block, half), F32), shape((width, block), F32)),
         in_specs=[scalars, scalars, far, VMEM, far, VMEM, VMEM, VMEM, VMEM, far, far],
         out_specs=(far, VMEM, VMEM),
         scratch_shapes=[
@@ -390,7 +391,7 @@
         name="program",
     )(clip_start, assign, enc_features, enc_gain, enc_kernel.reshape(3 * channels, channels), out_kernel.T,
       embed_weight.T, mod_scale, mod_shift, value_weight.reshape(n_e, block, half), value_cotangent.reshape(count, half))
-    return (values.reshape(value_cotangent.shape), grad_value, grad_embed)
+    return (values.reshape(value_cotangent.shape), grad_value, grad_embed.T)
 
 
 def solution(mesh):

time: 83.3 us -> 82.4 us (0.989)
  local copies, waits for them, and re-layouts: 5.03 us -> 4.15 us
    unnamed x5 -> x7, local copies, waits for them, and re-layouts: 5.03 us -> 4.15 us
where the time goes in v4:
time: 82.4 us; the launch traced here: 82.2 us
  Pallas kernels  77.4 us (94%)
  local copies, waits for them, and re-layouts  4.15 us (5%)
    pallas_call x1, Pallas kernels, local(): pl.pallas_call(functools.partial(program_kernel, n_e, n_f, frames, depth)...  77.4 us
    unnamed x7, local copies, waits for them, and re-layouts  4.15 us

profile of v4, /device:TPU:0, one launch (start us, length us, event | category | flops | bytes accessed | tf_op | source)
XLA Modules:
  0.0 82.2 jit_solution(1766627653382289087)
XLA Ops:
  0.6 77.4 %program.1 = (bf16[512,1536]{1,0:T(8,128)(2,1)}, f32[96,1536]{1,0:T(8,128)}, f32[64,96]{1,0:T(8,128)}) custom-call(s32[8]{0:T(128)} %start.1, s32[8]{0:T(128)} %assign.1, bf16[8,2,128,512]{3,2,1,0:T(8,128)(2,1)} %feat_hbm.1, f32[1,512]{1,0:T(1,128)} %gain.1, bf16[1536,512]{1,0:T(8,128)(2,1)} %bitcast.8, bf16[16,512]{1,0:T(8,128)(2,1)} %bitcast.13, ...), custom_call_target="tpu_custom_call" | custom-call | tf_op jit(solution)/shard_map/program/pallas_call | solution.py:369
  78.0 0.0 copy-start
  78.0 0.0 copy-start.1
  78.0 2.7 %copy.17 = bf16[1,2,256,1536]{3,2,1,0:T(8,128)(2,1)} copy(bf16[1,2,256,1536]{3,2,1,0:T(8,128)(2,1)} %bitcast.7) | data formatting | bytes 3145728
  80.7 0.0 copy-done
  80.7 0.8 copy.18
  81.6 0.0 copy-done.1
  81.6 0.6 copy.19
Async XLA Ops:
  78.0 2.7 %copy-start = (f32[96,1536]{1,0:T(8,128)S(1)}, f32[96,1536]{1,0:T(8,128)}, u32[]{:S(2)}) copy-start(f32[96,1536]{1,0:T(8,128)} %get-tuple-element.13) | copy-start | bytes 1769476
  78.0 3.5 %copy-start.1 = (f32[64,96]{1,0:T(8,128)S(1)}, f32[64,96]{1,0:T(8,128)}, u32[]{:S(2)}) copy-start(f32[64,96]{1,0:T(8,128)} %get-tuple-element.8) | copy-start | bytes 73732
